TPU v7x, 32 devices: a whole 2x2x4 slice. The times are simulated.
32 devices in a mesh: grp: 2 (over y), gy: 4 (over z), ch: 2 (over x), gx: 2 (over core).
Axes of the slice: x: 2, y: 2, z: 4, core: 2. Of those that a mesh axis runs over, the one named last changes fastest.
Arguments:
- activations: bfloat16 [384, 4, 8, 256], P('ch', 'grp', 'gy', 'gx'), parts along dimension 1, may hold values from -6 to 6
- weight: bfloat16 [27, 384, 384], P(None, 'ch'), may hold values from -0.0625 to 0.0625
- cotangent: bfloat16 [384, 4, 8, 256], P('ch', 'grp', 'gy', 'gx'), parts along dimension 1, may hold values from -6 to 6
- shear_shift: int32 [2], P('grp'), parts along dimension 0, may hold values from 0 to 255
Outputs:
- features: bfloat16 [384, 4, 8, 256], P('ch', 'grp', 'gy', 'gx'), parts along dimension 1
- input_grad: bfloat16 [384, 4, 8, 256], P('ch', 'grp', 'gy', 'gx'), parts along dimension 1
- weight_grad: float32 [54, 384, 384], P('grp', 'ch'), parts along dimension 0
There are 2 independent parts, one for each index of `grp`. A program takes and returns all parts, laid end to end along the dimension named above; an argument that names none is the same for every part. Nothing has to cross between parts.
Inputs may be any that keep to these rules, and one draw needn't show every extreme that they name: `shear_shift`: one offset for the group's snapshot.
All inputs are finite; a program needn't handle non-finite values.
Results may differ from a plain program's by a relative error of at most 0.001.
Values may be sent and summed in bfloat16 or wider, within the bound.
A program may use at most 128 MiB of HBM per device.

v0:
```python
import jax
import jax.numpy as jnp
from jax import lax
from jax.sharding import PartitionSpec as P


def extended_2(cells, sides, width):
    for axis, dim in sides:
        count = lax.axis_size(axis)
        head = lax.slice_in_dim(cells, 0, width, axis=dim)
        tail = lax.slice_in_dim(cells, cells.shape[dim] - width, cells.shape[dim], axis=dim)
        cells = jnp.concatenate(
            [
                lax.ppermute(tail, axis, [(i, (i + 1) % count) for i in range(count)]),
                cells,
                lax.ppermute(head, axis, [((i + 1) % count, i) for i in range(count)]),
            ],
            axis=dim,
        )
    return cells


def columns(extended, flipped, planes, y_cells, x_cells):
    stacked = []
    for z_step in range(3):
        for y_step in range(3):
            for x_step in range(3):
                if flipped:
                    z_from, y_from, x_from = (2 - z_step, 2 - y_step, 2 - x_step)
                else:
                    z_from, y_from, x_from = (z_step, y_step, x_step)
                window = extended[
                    :,
                    z_from : z_from + planes,
                    y_from : y_from + y_cells,
                    x_from : x_from + x_cells,
                ]
                stacked.append(window.reshape(extended.shape[0], -1))
    return jnp.stack(stacked).reshape(27 * extended.shape[0], -1)


def on_device(activations, weight, cotangent, shear_shift):
    local_ch, planes, y_cells, x_cells = activations.shape
    shift_value = shear_shift[0]
    joined = jnp.concatenate([activations, cotangent], 0)
    rimmed = extended_2(joined, (("gy", 2),), 1)
    whole = lax.all_gather(rimmed, "gx", axis=3, tiled=True)
    full_x = whole.shape[3]
    y_index = lax.axis_index("gy")
    y_count = lax.axis_size("gy")
    below = jnp.where(y_index == 0, jnp.roll(whole[:, :, :1], shift_value, axis=3), whole[:, :, :1])
    above = jnp.where(
        y_index == y_count - 1, jnp.roll(whole[:, :, -1:], -shift_value, axis=3), whole[:, :, -1:]
    )
    whole = jnp.concatenate([below, whole[:, :, 1:-1], above], 2)
    doubled = jnp.concatenate([whole, whole], 3)
    begin = (lax.axis_index("gx") * x_cells - 1 + full_x) % full_x
    window = lax.dynamic_slice_in_dim(doubled, begin, x_cells + 2, 3)
    window = jnp.pad(window, ((0, 0), (1, 1), (0, 0), (0, 0)))
    input_ext = window[:local_ch]
    cotan_ext = window[local_ch:]
    cotan_flat = cotangent.reshape(local_ch, -1)
    panel = lax.all_gather(input_ext, "ch", axis=0, tiled=True)
    amount = panel.shape[0]
    cols = columns(panel, False, planes, y_cells, x_cells)
    kernel = weight
    kernel_flat = jnp.transpose(kernel, (1, 0, 2)).reshape(local_ch, 27 * amount)
    out_acc = jnp.dot(kernel_flat, cols, preferred_element_type=jnp.float32)
    grad_flat = lax.dot_general(
        cotan_flat, cols, (((1,), (1,)), ((), ())), preferred_element_type=jnp.float32
    )
    grad_part = jnp.transpose(grad_flat.reshape(local_ch, 27, amount), (1, 0, 2))
    grad_acc = grad_part
    out_acc, grad_acc = (out_acc, grad_acc)
    cotan_cols = columns(cotan_ext, True, planes, y_cells, x_cells)
    amount = local_ch * lax.axis_size("ch")
    kernel = weight.reshape(27 * local_ch, amount)
    term = lax.dot_general(
        kernel, cotan_cols, (((0,), (0,)), ((), ())), preferred_element_type=jnp.float32
    )
    grad_in = lax.psum_scatter(
        term.reshape(amount, planes, y_cells, x_cells), "ch", scatter_dimension=0, tiled=True
    )
    grad_sum = lax.psum(grad_acc, ("gy", "gx"))
    scale = float(planes * y_cells * y_count * x_cells * lax.axis_size("gx")) ** (-0.5)
    features = out_acc.reshape(local_ch, planes, y_cells, x_cells).astype(jnp.bfloat16)
    return (features, grad_in.astype(jnp.bfloat16), grad_sum * scale)


def solution(mesh):
    return jax.shard_map(
        on_device,
        mesh=mesh,
        in_specs=(
            P("ch", "grp", "gy", "gx"),
            P(None, "ch", None),
            P("ch", "grp", "gy", "gx"),
            P("grp"),
        ),
        out_specs=(P("ch", "grp", "gy", "gx"), P("ch", "grp", "gy", "gx"), P("grp", "ch", None)),
        check_vma=False,
    )
```

profile of v0, /device:TPU:0, one launch (start us, length us, event | category | flops | bytes accessed | tf_op | source)
XLA Modules:
  0.0 466.8 jit_solution(1102423540821568638)
XLA Ops:
  10.0 3.1 collective-permute-start
  13.1 2.1 collective-permute-start.1
  15.2 9.9 %collective-permute-done = bf16[384,2,1,128]{3,2,1,0:T(2,128)(2,1)S(1)} collective-permute-done((bf16[384,2,1,128]{3,2,1,0:T(2,128)(2,1)S(1)}, bf16[384,2,1,128]{3,2,1,0:T(2,128)(2,1)S(1)}, u32[]{:S(2)}, u32[]{:S(2)}) %collective-permute-start) | collective-permute-done | bytes 196640 | tf_op jit(solution)/shard_map/ppermute | solution.py:14
  25.1 7.0 %collective-permute-done.1 = bf16[384,2,1,128]{3,2,1,0:T(2,128)(2,1)S(1)} collective-permute-done((bf16[384,2,1,128]{3,2,1,0:T(2,128)(2,1)S(1)}, bf16[384,2,1,128]{3,2,1,0:T(2,128)(2,1)S(1)}, u32[]{:S(2)}, u32[]{:S(2)}) %collective-permute-start.1) | collective-permute-done | bytes 196640 | tf_op jit(solution)/shard_map/ppermute | solution.py:16
  32.1 2.2 pad_maximum_fusion
  37.6 6.5 %all-gather.3.cloned.1.call-done = bf16[384,2,4,256]{3,2,1,0:T(4,128)(2,1)} async-done(((bf16[384,2,4,128]{3,2,1,0:T(4,128)(2,1)}), bf16[384,2,4,256]{3,2,1,0:T(4,128)(2,1)}) %all-gather.3.cloned.1.call-update) | async-done | bytes 1572880 | tf_op jit(solution)/shard_map/all_gather | solution.py:47
  44.1 3.4 fusion.21
  47.5 7.1 %broadcast_select_fusion = (bf16[384,2,1,256]{3,2,1,0:T(2,128)(2,1)S(1)}, bf16[384,2,1,256]{3,2,1,0:T(2,128)(2,1)S(1)}) fusion(bf16[384,2,1,256]{3,2,1,0:T(2,128)(2,1)S(1)} %get-tuple-element.64, pred[]{:T(512)S(6)} %eq.11, s32[]{:T(128)S(6)} %select_n.44, bf16[384,2,1,256]{3,2,1,0:T(2,128)(2,1)S(1)} %get-tuple-element.65, s32[]{:T(128)S(6)} %select_n.42, ...), kind=kLoop, calls=%fused_computation.38 | loop fusion | flops 1966080 | bytes 1572874 | tf_op jit(solution)/shard_map/jit(_where)/select_n | solution.py:52
  55.4 11.8 %fusion.4 = bf16[384,2,4,130]{3,2,1,0:T(4,128)(2,1)S(1)} fusion(s32[]{:T(128)S(6)} %select_n.38, bf16[384,2,1,256]{3,2,1,0:T(2,128)(2,1)S(1)} %get-tuple-element.69, bf16[384,2,2,256]{3,2,1,0:T(2,128)(2,1)S(1)} %slice.282, bf16[384,2,1,256]{3,2,1,0:T(2,128)(2,1)S(1)} %get-tuple-element.68), kind=kLoop, calls=%fused_computation.31 | loop fusion | flops 4792320 | bytes 2371588 | tf_op jit(solution)/shard_map/concatenate | solution.py:56
  67.2 4.2 pad_slice_fusion
  71.5 2.7 fusion.20
  74.2 1.7 pad_slice_fusion.18
  75.9 1.7 stack_reshape.189
  77.6 1.6 constant_dynamic-update-slice_fusion.55
  85.3 1.7 stack_reshape.198
  100.8 1.6 constant_dynamic-update-slice_fusion.54
  102.4 1.6 constant_dynamic-update-slice_fusion.53
  104.1 1.6 constant_dynamic-update-slice_fusion.52
  115.6 31.4 %all-gather.5.cloned.1.call-done = bf16[384,4,4,130]{3,2,1,0:T(4,128)(2,1)} async-done(((bf16[192,4,4,130]{3,2,1,0:T(4,128)(2,1)}), bf16[384,4,4,130]{3,2,1,0:T(4,128)(2,1)}) %all-gather.5.cloned.1.call-update) | async-done | bytes 1597456 | tf_op jit(solution)/shard_map/all_gather | solution.py:63
  147.0 9.2 %fusion.19 = (bf16[384,2,2,128]{3,2,1,0:T(2,128)(2,1)}, bf16[384,2,2,128]{3,2,1,0:T(2,128)(2,1)}, bf16[384,2,2,128]{3,2,1,0:T(2,128)(2,1)S(1)}, bf16[384,2,2,128...) fusion(bf16[384,4,4,130]{3,2,1,0:T(4,128)(2,1)} %all-gather.5.c, ...), kind=kLoop, calls=%fused_computation.104 | loop fusion | bytes 6291456 | tf_op jit(solution)/shard_map/slice | solution.py:32
  156.3 1.9 stack_reshape.162
  158.2 1.8 constant_dynamic-update-slice_fusion.28
  159.9 1.9 stack_reshape.163
  161.8 1.9 stack_reshape.164
  163.7 1.9 stack_reshape.165
  165.6 1.9 stack_reshape.166
  169.6 1.9 stack_reshape.169
  171.5 10.1 %fusion.18 = (bf16[384,2,2,128]{3,2,1,0:T(2,128)(2,1)}, bf16[384,2,2,128]{3,2,1,0:T(2,128)(2,1)}, bf16[384,2,2,128]{3,2,1,0:T(2,128)(2,1)}, bf16[384,2,2,128]{3,...) fusion(bf16[384,4,4,130]{3,2,1,0:T(4,128)(2,1)S(1)} %copy-done), kind=kLoop, calls=%fused_computation.103 | loop fusion | bytes 14942208 | tf_op jit(solution)/shard_map/slice | solution.py:32
  181.6 2.0 stack_reshape.170
  183.7 1.9 stack_reshape.171
  185.6 1.9 stack_reshape.172
  187.5 1.9 stack_reshape.173
  189.4 1.9 stack_reshape.174
  191.4 1.9 stack_reshape.175
  193.3 2.0 stack_reshape.176
  197.9 1.9 stack_reshape.180
  200.8 2.0 stack_reshape.182
  202.8 1.9 stack_reshape.183
  204.7 1.9 stack_reshape.184
  206.6 1.9 stack_reshape.185
  231.4 11.0 %convolution_bitcast_fusion = f32[192,10368]{1,0:T(8,128)} fusion(bf16[10368,512]{1,0:T(8,128)(2,1)} %bitcast.38, bf16[192,512]{1,0:T(8,128)(2,1)S(1)} %copy-done.31), kind=kOutput, calls=%fused_computation | convolution fusion | flops 2038431744 | bytes 18776064 | tf_op jit(solution)/shard_map/dot_general | solution.py:69
  242.3 9.4 %reshape.26 = f32[192,27,384]{2,1,0:T(8,128)} reshape(f32[192,10368]{1,0:T(8,128)} %convolution_bitcast_fusion) | data formatting | bytes 15925248 | tf_op jit(solution)/shard_map/reshape | solution.py:72
  259.6 6.2 %fusion.23 = f32[512,384,1]{1,0,2:T(8,128)S(1)} fusion(bf16[27,192,512]{2,1,0:T(8,128)(2,1)} %constant_dynamic-update-slice_fusion.29, bf16[27,192,384]{2,1,0:T(8,128)(2,1)} %param.7), kind=kOutput, calls=%fused_computation.108 | convolution fusion | flops 2038431744 | bytes 10076160 | tf_op jit(solution)/shard_map/dot_general | solution.py:78
  266.5 22.7 %all-reduce.6 = bf16[384,2,2,128]{3,2,1,0:T(2,128)(2,1)S(1)} all-reduce(f32[384,2,2,128]{3,2,1,0:T(2,128)S(1)} %copy.11), channel_id=2, replica_groups=mesh['grp'=2,'gy'=4,'ch'=2,'gx'=2] {'ch'}, use_global_device_ids=true, to_apply=%region_0.2.clone | all-reduce | flops 196608 | bytes 1179648
  290.0 7.6 %fusion.13 = bf16[192,512]{1,0:T(8,128)(2,1)S(1)} fusion(bf16[27,384,512]{2,1,0:T(8,128)(2,1)} %constant_dynamic-update-slice_fusion.2, bf16[27,192,384]{2,1,0:T(8,128)(2,1)} %param.7), kind=kOutput, calls=%fused_computation.42 | convolution fusion | flops 2038530048 | bytes 14794752 | tf_op jit(solution)/shard_map/dot_general | solution.py:68
  298.3 149.0 %all-reduce.5.cloned.1.call-done = f32[27,192,384]{2,0,1:T(8,128)} async-done(((f32[27,192,384]{2,0,1:T(8,128)}), f32[27,192,384]{2,0,1:T(8,128)}) %all-reduce.5.cloned.1.call-update) | async-done | bytes 7962640 | tf_op jit(solution)/shard_map/psum | solution.py:84
  447.3 4.8 %broadcast_multiply_fusion = f32[27,192,384]{2,0,1:T(8,128)S(1)} fusion(f32[27,192,384]{2,0,1:T(8,128)} %all-reduce.5.cloned.1.call-done), kind=kLoop, calls=%fused_computation.1 | loop fusion | flops 1990656 | bytes 15925248 | tf_op jit(solution)/shard_map/mul | solution.py:87
  452.1 7.9 %copy.12 = f32[27,192,384]{2,1,0:T(8,128)} copy(f32[27,192,384]{2,0,1:T(8,128)S(1)} %broadcast_multiply_fusion) | data formatting | bytes 15925248
  (198 shorter events, 73.8 us)
Async XLA Ops:
  7.2 29.2 %copy-start.49 = (u32[32]{0:T(128)S(1)}, u32[32]{0:T(128)}, u32[]{:S(2)}) copy-start(u32[32]{0:T(128)} %constant.60) | copy-start | bytes 388
  7.2 28.4 %copy-start.33 = (bf16[192,2,2,128]{3,2,1,0:T(2,128)(2,1)S(1)}, bf16[192,2,2,128]{3,2,1,0:T(2,128)(2,1)}, u32[]{:S(2)}) copy-start(bf16[192,2,2,128]{3,2,1,0:T(2,128)(2,1)} %param.8) | copy-start | bytes 589828
  7.2 36.9 %all-gather.3.cloned.1.call-start = ((), (), s32[]{:S(2)}) async-start(), calls=%async_computation | async-start | bytes 2359296 | tf_op jit(solution)/shard_map/all_gather | solution.py:47
  10.0 15.1 %collective-permute-start = (bf16[384,2,1,128]{3,2,1,0:T(2,128)(2,1)S(1)}, bf16[384,2,1,128]{3,2,1,0:T(2,128)(2,1)S(1)}, u32[]{:S(2)}, u32[]{:S(2)}) collective-permute-start(bf16[384,2,1,128]{3,2,1,0:T(2,128)(2,1)S(1)} %get-tuple-element.66), channel_id=1, source_target_pairs={{0,4},{4,8},{8,12},{12,0},{1,5},{5,9},{9,13},{13,1},{2,6},{6,10},{... | collective-permute-start | bytes 589832 | tf_op jit(solution)/shard_map/ppermute | solution.py:14
  13.1 19.0 %collective-permute-start.1 = (bf16[384,2,1,128]{3,2,1,0:T(2,128)(2,1)S(1)}, bf16[384,2,1,128]{3,2,1,0:T(2,128)(2,1)S(1)}, u32[]{:S(2)}, u32[]{:S(2)}) collective-permute-start(bf16[384,2,1,128]{3,2,1,0:T(2,128)(2,1)S(1)} %get-tuple-element.67), channel_id=1, source_target_pairs={{4,0},{8,4},{12,8},{0,12},{5,1},{9,5},{13,9},{1,13},{6,2},{10,6},{... | collective-permute-start | bytes 589832 | tf_op jit(solution)/shard_map/ppermute | solution.py:16
  34.3 112.7 %all-gather.5.cloned.1.call-start = ((), (), s32[]{:S(2)}) async-start(), calls=%async_computation.1 | async-start | bytes 4718592 | tf_op jit(solution)/shard_map/all_gather | solution.py:63
  44.1 10.5 %copy-start.1 = (bf16[384,2,4,256]{3,2,1,0:T(4,128)(2,1)S(1)}, bf16[384,2,4,256]{3,2,1,0:T(4,128)(2,1)}, u32[]{:S(2)}) copy-start(bf16[384,2,4,256]{3,2,1,0:T(4,128)(2,1)} %all-gather.3.cloned.1.call-done) | copy-start | bytes 4718596
  79.9 13.2 %copy-start.32 = (bf16[192,2,2,128]{3,2,1,0:T(2,128)(2,1)S(1)}, bf16[192,2,2,128]{3,2,1,0:T(2,128)(2,1)}, u32[]{:S(2)}) copy-start(bf16[192,2,2,128]{3,2,1,0:T(2,128)(2,1)} %get-tuple-element.56) | copy-start | bytes 589828
  93.2 16.9 %copy-start.44 = (bf16[1,192,512]{2,1,0:T(8,128)(2,1)S(1)}, bf16[1,192,512]{2,1,0:T(8,128)(2,1)}, u32[]{:S(2)}) copy-start(bf16[1,192,512]{2,1,0:T(8,128)(2,1)} %stack_reshape.198) | copy-start | bytes 589828
  93.9 15.5 %copy-start.45 = (bf16[1,192,512]{2,1,0:T(8,128)(2,1)S(1)}, bf16[1,192,512]{2,1,0:T(8,128)(2,1)}, u32[]{:S(2)}) copy-start(bf16[1,192,512]{2,1,0:T(8,128)(2,1)} %stack_reshape.197) | copy-start | bytes 589828
  94.7 14.0 %copy-start.46 = (bf16[1,192,512]{2,1,0:T(8,128)(2,1)S(1)}, bf16[1,192,512]{2,1,0:T(8,128)(2,1)}, u32[]{:S(2)}) copy-start(bf16[1,192,512]{2,1,0:T(8,128)(2,1)} %stack_reshape.196) | copy-start | bytes 589828
  95.4 12.6 %copy-start.47 = (bf16[1,192,512]{2,1,0:T(8,128)(2,1)S(1)}, bf16[1,192,512]{2,1,0:T(8,128)(2,1)}, u32[]{:S(2)}) copy-start(bf16[1,192,512]{2,1,0:T(8,128)(2,1)} %stack_reshape.195) | copy-start | bytes 589828
  96.2 11.1 %copy-start.48 = (bf16[1,192,512]{2,1,0:T(8,128)(2,1)S(1)}, bf16[1,192,512]{2,1,0:T(8,128)(2,1)}, u32[]{:S(2)}) copy-start(bf16[1,192,512]{2,1,0:T(8,128)(2,1)} %stack_reshape.194) | copy-start | bytes 589828
  100.8 346.5 %all-reduce.5.cloned.1.call-start = ((), (), s32[]{:S(2)}) async-start(), calls=%async_computation.2 | async-start | bytes 18874368 | tf_op jit(solution)/shard_map/psum | solution.py:84
  147.0 24.5 %copy-start = (bf16[384,4,4,130]{3,2,1,0:T(4,128)(2,1)S(1)}, bf16[384,4,4,130]{3,2,1,0:T(4,128)(2,1)}, u32[]{:S(2)}) copy-start(bf16[384,4,4,130]{3,2,1,0:T(4,128)(2,1)} %all-gather.5.cloned.1.call-done) | copy-start | bytes 4792324
  181.6 13.6 %copy-start.30 = (bf16[384,2,2,128]{3,2,1,0:T(2,128)(2,1)S(1)}, bf16[384,2,2,128]{3,2,1,0:T(2,128)(2,1)}, u32[]{:S(2)}) copy-start(bf16[384,2,2,128]{3,2,1,0:T(2,128)(2,1)} %get-tuple-element.21) | copy-start | bytes 1179652
  181.6 14.5 %copy-start.29 = (bf16[384,2,2,128]{3,2,1,0:T(2,128)(2,1)S(1)}, bf16[384,2,2,128]{3,2,1,0:T(2,128)(2,1)}, u32[]{:S(2)}) copy-start(bf16[384,2,2,128]{3,2,1,0:T(2,128)(2,1)} %get-tuple-element.20) | copy-start | bytes 1179652
  181.6 15.4 %copy-start.28 = (bf16[384,2,2,128]{3,2,1,0:T(2,128)(2,1)S(1)}, bf16[384,2,2,128]{3,2,1,0:T(2,128)(2,1)}, u32[]{:S(2)}) copy-start(bf16[384,2,2,128]{3,2,1,0:T(2,128)(2,1)} %get-tuple-element.19) | copy-start | bytes 1179652
  181.6 18.2 %copy-start.27 = (bf16[384,2,2,128]{3,2,1,0:T(2,128)(2,1)S(1)}, bf16[384,2,2,128]{3,2,1,0:T(2,128)(2,1)}, u32[]{:S(2)}) copy-start(bf16[384,2,2,128]{3,2,1,0:T(2,128)(2,1)} %get-tuple-element.17) | copy-start | bytes 1179652
  187.5 21.0 %copy-start.26 = (bf16[384,2,2,128]{3,2,1,0:T(2,128)(2,1)S(1)}, bf16[384,2,2,128]{3,2,1,0:T(2,128)(2,1)}, u32[]{:S(2)}) copy-start(bf16[384,2,2,128]{3,2,1,0:T(2,128)(2,1)} %get-tuple-element.12) | copy-start | bytes 1179652
  189.4 20.0 %copy-start.25 = (bf16[384,2,2,128]{3,2,1,0:T(2,128)(2,1)S(1)}, bf16[384,2,2,128]{3,2,1,0:T(2,128)(2,1)}, u32[]{:S(2)}) copy-start(bf16[384,2,2,128]{3,2,1,0:T(2,128)(2,1)} %get-tuple-element.11) | copy-start | bytes 1179652
  193.3 17.4 %copy-start.6 = (bf16[1,384,512]{2,1,0:T(8,128)(2,1)S(1)}, bf16[1,384,512]{2,1,0:T(8,128)(2,1)}, u32[]{:S(2)}) copy-start(bf16[1,384,512]{2,1,0:T(8,128)(2,1)} %stack_reshape.163) | copy-start | bytes 1179652
  195.2 16.3 %copy-start.7 = (bf16[1,384,512]{2,1,0:T(8,128)(2,1)S(1)}, bf16[1,384,512]{2,1,0:T(8,128)(2,1)}, u32[]{:S(2)}) copy-start(bf16[1,384,512]{2,1,0:T(8,128)(2,1)} %stack_reshape.164) | copy-start | bytes 1179652
  196.1 16.2 %copy-start.5 = (bf16[1,384,512]{2,1,0:T(8,128)(2,1)S(1)}, bf16[1,384,512]{2,1,0:T(8,128)(2,1)}, u32[]{:S(2)}) copy-start(bf16[1,384,512]{2,1,0:T(8,128)(2,1)} %stack_reshape.165) | copy-start | bytes 1179652
  197.0 16.1 %copy-start.4 = (bf16[1,384,512]{2,1,0:T(8,128)(2,1)S(1)}, bf16[1,384,512]{2,1,0:T(8,128)(2,1)}, u32[]{:S(2)}) copy-start(bf16[1,384,512]{2,1,0:T(8,128)(2,1)} %stack_reshape.166) | copy-start | bytes 1179652
  197.9 16.0 %copy-start.3 = (bf16[1,384,512]{2,1,0:T(8,128)(2,1)S(1)}, bf16[1,384,512]{2,1,0:T(8,128)(2,1)}, u32[]{:S(2)}) copy-start(bf16[1,384,512]{2,1,0:T(8,128)(2,1)} %stack_reshape.167) | copy-start | bytes 1179652
  200.8 14.7 %copy-start.2 = (bf16[1,384,512]{2,1,0:T(8,128)(2,1)S(1)}, bf16[1,384,512]{2,1,0:T(8,128)(2,1)}, u32[]{:S(2)}) copy-start(bf16[1,384,512]{2,1,0:T(8,128)(2,1)} %stack_reshape.169) | copy-start | bytes 1179652
  210.7 5.6 %copy-start.24 = (bf16[1,384,512]{2,1,0:T(8,128)(2,1)S(1)}, bf16[1,384,512]{2,1,0:T(8,128)(2,1)}, u32[]{:S(2)}) copy-start(bf16[1,384,512]{2,1,0:T(8,128)(2,1)} %stack_reshape.170) | copy-start | bytes 1179652
  210.7 6.4 %copy-start.23 = (bf16[1,384,512]{2,1,0:T(8,128)(2,1)S(1)}, bf16[1,384,512]{2,1,0:T(8,128)(2,1)}, u32[]{:S(2)}) copy-start(bf16[1,384,512]{2,1,0:T(8,128)(2,1)} %stack_reshape.171) | copy-start | bytes 1179652
  210.7 7.1 %copy-start.22 = (bf16[1,384,512]{2,1,0:T(8,128)(2,1)S(1)}, bf16[1,384,512]{2,1,0:T(8,128)(2,1)}, u32[]{:S(2)}) copy-start(bf16[1,384,512]{2,1,0:T(8,128)(2,1)} %stack_reshape.172) | copy-start | bytes 1179652
  210.7 7.9 %copy-start.21 = (bf16[1,384,512]{2,1,0:T(8,128)(2,1)S(1)}, bf16[1,384,512]{2,1,0:T(8,128)(2,1)}, u32[]{:S(2)}) copy-start(bf16[1,384,512]{2,1,0:T(8,128)(2,1)} %stack_reshape.173) | copy-start | bytes 1179652
  210.7 8.7 %copy-start.20 = (bf16[1,384,512]{2,1,0:T(8,128)(2,1)S(1)}, bf16[1,384,512]{2,1,0:T(8,128)(2,1)}, u32[]{:S(2)}) copy-start(bf16[1,384,512]{2,1,0:T(8,128)(2,1)} %stack_reshape.174) | copy-start | bytes 1179652
  210.7 9.5 %copy-start.19 = (bf16[1,384,512]{2,1,0:T(8,128)(2,1)S(1)}, bf16[1,384,512]{2,1,0:T(8,128)(2,1)}, u32[]{:S(2)}) copy-start(bf16[1,384,512]{2,1,0:T(8,128)(2,1)} %stack_reshape.175) | copy-start | bytes 1179652
  210.7 10.2 %copy-start.18 = (bf16[1,384,512]{2,1,0:T(8,128)(2,1)S(1)}, bf16[1,384,512]{2,1,0:T(8,128)(2,1)}, u32[]{:S(2)}) copy-start(bf16[1,384,512]{2,1,0:T(8,128)(2,1)} %stack_reshape.176) | copy-start | bytes 1179652
  211.6 10.2 %copy-start.17 = (bf16[1,384,512]{2,1,0:T(8,128)(2,1)S(1)}, bf16[1,384,512]{2,1,0:T(8,128)(2,1)}, u32[]{:S(2)}) copy-start(bf16[1,384,512]{2,1,0:T(8,128)(2,1)} %stack_reshape.177) | copy-start | bytes 1179652
  212.3 10.3 %copy-start.16 = (bf16[1,384,512]{2,1,0:T(8,128)(2,1)S(1)}, bf16[1,384,512]{2,1,0:T(8,128)(2,1)}, u32[]{:S(2)}) copy-start(bf16[1,384,512]{2,1,0:T(8,128)(2,1)} %stack_reshape.178) | copy-start | bytes 1179652
  213.1 10.3 %copy-start.15 = (bf16[1,384,512]{2,1,0:T(8,128)(2,1)S(1)}, bf16[1,384,512]{2,1,0:T(8,128)(2,1)}, u32[]{:S(2)}) copy-start(bf16[1,384,512]{2,1,0:T(8,128)(2,1)} %stack_reshape.179) | copy-start | bytes 1179652
  213.9 10.3 %copy-start.14 = (bf16[1,384,512]{2,1,0:T(8,128)(2,1)S(1)}, bf16[1,384,512]{2,1,0:T(8,128)(2,1)}, u32[]{:S(2)}) copy-start(bf16[1,384,512]{2,1,0:T(8,128)(2,1)} %stack_reshape.180) | copy-start | bytes 1179652
  214.7 10.3 %copy-start.13 = (bf16[1,384,512]{2,1,0:T(8,128)(2,1)S(1)}, bf16[1,384,512]{2,1,0:T(8,128)(2,1)}, u32[]{:S(2)}) copy-start(bf16[1,384,512]{2,1,0:T(8,128)(2,1)} %stack_reshape.181) | copy-start | bytes 1179652
  215.5 10.3 %copy-start.12 = (bf16[1,384,512]{2,1,0:T(8,128)(2,1)S(1)}, bf16[1,384,512]{2,1,0:T(8,128)(2,1)}, u32[]{:S(2)}) copy-start(bf16[1,384,512]{2,1,0:T(8,128)(2,1)} %stack_reshape.182) | copy-start | bytes 1179652
  216.3 10.4 %copy-start.11 = (bf16[1,384,512]{2,1,0:T(8,128)(2,1)S(1)}, bf16[1,384,512]{2,1,0:T(8,128)(2,1)}, u32[]{:S(2)}) copy-start(bf16[1,384,512]{2,1,0:T(8,128)(2,1)} %stack_reshape.183) | copy-start | bytes 1179652
  217.1 10.4 %copy-start.10 = (bf16[1,384,512]{2,1,0:T(8,128)(2,1)S(1)}, bf16[1,384,512]{2,1,0:T(8,128)(2,1)}, u32[]{:S(2)}) copy-start(bf16[1,384,512]{2,1,0:T(8,128)(2,1)} %stack_reshape.184) | copy-start | bytes 1179652
  217.8 10.4 %copy-start.9 = (bf16[1,384,512]{2,1,0:T(8,128)(2,1)S(1)}, bf16[1,384,512]{2,1,0:T(8,128)(2,1)}, u32[]{:S(2)}) copy-start(bf16[1,384,512]{2,1,0:T(8,128)(2,1)} %stack_reshape.185) | copy-start | bytes 1179652
  218.6 10.4 %copy-start.8 = (bf16[1,384,512]{2,1,0:T(8,128)(2,1)S(1)}, bf16[1,384,512]{2,1,0:T(8,128)(2,1)}, u32[]{:S(2)}) copy-start(bf16[1,384,512]{2,1,0:T(8,128)(2,1)} %stack_reshape.186) | copy-start | bytes 1179652
  221.0 10.4 %copy-start.31 = (bf16[192,512]{1,0:T(8,128)(2,1)S(1)}, bf16[192,512]{1,0:T(8,128)(2,1)}, u32[]{:S(2)}) copy-start(bf16[192,512]{1,0:T(8,128)(2,1)} %reshape.25) | copy-start | bytes 589828
  251.8 5.8 %copy-start.36 = (bf16[1,192,512]{2,1,0:T(8,128)(2,1)S(1)}, bf16[1,192,512]{2,1,0:T(8,128)(2,1)}, u32[]{:S(2)}) copy-start(bf16[1,192,512]{2,1,0:T(8,128)(2,1)} %stack_reshape.213) | copy-start | bytes 589828
  251.8 6.4 %copy-start.34 = (bf16[1,192,512]{2,1,0:T(8,128)(2,1)S(1)}, bf16[1,192,512]{2,1,0:T(8,128)(2,1)}, u32[]{:S(2)}) copy-start(bf16[1,192,512]{2,1,0:T(8,128)(2,1)} %stack_reshape.214) | copy-start | bytes 589828
  251.8 7.1 %copy-start.35 = (bf16[1,192,512]{2,1,0:T(8,128)(2,1)S(1)}, bf16[1,192,512]{2,1,0:T(8,128)(2,1)}, u32[]{:S(2)}) copy-start(bf16[1,192,512]{2,1,0:T(8,128)(2,1)} %stack_reshape.215) | copy-start | bytes 589828
  (7 other events, 21.0 us)
Sparse Core Ops, SparseCore 0:
  34.4 9.6 all-gather.2
  100.9 46.0 all-gather.4
  251.9 195.3 all-reduce.4
where the time goes:
time: 471 us; the launch traced here: 467 us
  waiting for transfers between devices  204 us (43%)
  local copies, waits for them, and re-layouts  168 us (36%)
  other arithmetic  25.9 us (5%)
  matrix products  24.7 us (5%)
  blocking collectives  22.7 us (5%)
  between operations  15.8 us (3%)
  starting transfers between devices  5.81 us (1%)
    psum x1, waiting for transfers between devices, on_device(): grad_sum = lax.psum(grad_acc, ('gy', 'gx'))  149 us
    another operation x56, local copies, waits for them, and re-layouts, columns(): return jnp.stack(stacked).reshape(27 * extended.shape[0], -1)  67.1 us
    unnamed x155, local copies, waits for them, and re-layouts  54.7 us
    all_gather x1, waiting for transfers between devices, on_device(): panel = lax.all_gather(input_ext, 'ch', axis=0, tiled=True)  31.4 us
    slice x4, local copies, waits for them, and re-layouts, columns(): extended[:, z_from:z_from + planes, y_from:y_from + y_cells, x_from:x_fro...  26.2 us
    unnamed x1, blocking collectives  22.7 us
    concatenate x1, other arithmetic, on_device(): doubled = jnp.concatenate([whole, whole], 3)  11.8 us
    dot_general x1, matrix products, on_device(): lax.dot_general(cotan_flat, cols, (((1,), (1,)), ((), ())), preferred_ele...  11 us
  transfers between devices with their start and end apart: 5, of which 5 were waited for; matrix products, arithmetic and copies ran while one was open for 8% of the time, Pallas kernels for 0%

commit v1 on v0

v1 whole, which is shorter than its diff:
```python
import functools

import jax
import jax.numpy as jnp
from jax import lax
from jax.experimental import pallas as pl
from jax.experimental.pallas import tpu as pltpu
from jax.sharding import PartitionSpec as P

BF16 = jnp.bfloat16
F32 = jnp.float32
LIMIT = 56 * 1024 * 1024


def gather_kernel(n, nch, a_ref, t_ref, buf, loc_sem, zs_sem, zr_sem, xs_sem, xr_sem, cs_sem, cr_sem):
    q = lax.axis_index("gy")
    h = lax.axis_index("ch")
    c = lax.axis_index("gx")
    other = 1 - c

    barrier = pltpu.get_barrier_semaphore()

    @pl.when(q > 0)
    def _():
        pl.semaphore_signal(barrier, inc=1, device_id={"gy": q - 1}, device_id_type=pl.DeviceIdType.MESH)

    @pl.when(q < n - 1)
    def _():
        pl.semaphore_signal(barrier, inc=1, device_id={"gy": q + 1}, device_id_type=pl.DeviceIdType.MESH)

    for d in range(1, nch):
        pl.semaphore_signal(
            barrier, inc=1, device_id={"ch": lax.rem(h + d, nch)}, device_id_type=pl.DeviceIdType.MESH
        )
    pl.semaphore_signal(barrier, inc=1, device_id={"gx": other}, device_id_type=pl.DeviceIdType.MESH)
    own_a = pltpu.make_async_copy(a_ref, buf.at[q, c, h], loc_sem.at[0])
    own_t = pltpu.make_async_copy(t_ref, buf.at[q, c, nch], loc_sem.at[1])
    own_a.start()
    own_t.start()
    own_a.wait()
    own_t.wait()
    edges = jnp.where(q > 0, 1, 0) + jnp.where(q < n - 1, 1, 0)
    pl.semaphore_wait(barrier, edges + nch)

    def z_copy(step, direction, kind, source):
        slot = buf.at[source, c, h if kind == 0 else nch]
        return pltpu.make_async_remote_copy(
            src_ref=slot,
            dst_ref=slot,
            send_sem=zs_sem.at[direction, step, kind],
            recv_sem=zr_sem.at[direction, step, kind],
            device_id={"gy": q - 1 if direction == 0 else q + 1},
            device_id_type=pl.DeviceIdType.MESH,
        )

    def x_copy(source, d):
        slot = buf.at[source, c, h]
        return pltpu.make_async_remote_copy(
            src_ref=slot,
            dst_ref=slot,
            send_sem=xs_sem.at[source, d],
            recv_sem=xr_sem.at[source, d],
            device_id={"ch": lax.rem(h + d, nch)},
            device_id_type=pl.DeviceIdType.MESH,
        )

    def x_arrival(source, d):
        slot = buf.at[source, c, lax.rem(h - d + nch, nch)]
        return pltpu.make_async_remote_copy(
            src_ref=slot,
            dst_ref=slot,
            send_sem=xs_sem.at[source, d],
            recv_sem=xr_sem.at[source, d],
            device_id={"ch": lax.rem(h + d, nch)},
            device_id_type=pl.DeviceIdType.MESH,
        )

    def c_copy(source, d, side):
        kind = nch if d == nch else lax.rem(h - d + nch, nch)
        slot = buf.at[source, side, kind]
        return pltpu.make_async_remote_copy(
            src_ref=slot,
            dst_ref=slot,
            send_sem=cs_sem.at[source, d],
            recv_sem=cr_sem.at[source, d],
            device_id={"gx": other},
            device_id_type=pl.DeviceIdType.MESH,
        )

    def forward(source):
        for d in range(1, nch):
            x_copy(source, d).start()
        c_copy(source, 0, c).start()
        c_copy(source, nch, c).start()

    def relay(source):
        for d in range(1, nch):
            x_arrival(source, d).wait_recv()
            c_copy(source, d, c).start()

    for step in range(n - 1):
        down = (q >= 1) & (q + step < n)
        up = (q + 1 < n) & (q - step >= 0)

        @pl.when(down)
        def _():
            for kind in range(2):
                z_copy(step, 0, kind, q + step).start()

        @pl.when(up)
        def _():
            for kind in range(2):
                z_copy(step, 1, kind, q - step).start()

        if step == 0:
            forward(q)
            relay(q)
        else:

            @pl.when(q + step < n)
            def _():
                forward(q + step)
                relay(q + step)

            @pl.when(q - step >= 0)
            def _():
                forward(q - step)
                relay(q - step)

        @pl.when(q + step + 1 < n)
        def _():
            for kind in range(2):
                z_copy(step, 0, kind, q + step + 1).wait_recv()

        @pl.when(q - step - 1 >= 0)
        def _():
            for kind in range(2):
                z_copy(step, 1, kind, q - step - 1).wait_recv()

    @pl.when(q == 0)
    def _():
        forward(q + n - 1)
        relay(q + n - 1)

    @pl.when(q == n - 1)
    def _():
        forward(q - (n - 1))
        relay(q - (n - 1))

    for step in range(n - 1):

        @pl.when((q >= 1) & (q + step < n))
        def _():
            for kind in range(2):
                z_copy(step, 0, kind, q + step).wait_send()

        @pl.when((q + 1 < n) & (q - step >= 0))
        def _():
            for kind in range(2):
                z_copy(step, 1, kind, q - step).wait_send()

    for source in range(n):
        for d in range(1, nch):
            x_copy(source, d).wait_send()
        for d in range(nch + 1):
            c_copy(source, d, c).wait_send()
            c_copy(source, d, other).wait_recv()


def gather(n, nch, mine_a, mine_t):
    pieces, local_ch, x_cells = mine_a.shape
    return pl.pallas_call(
        functools.partial(gather_kernel, n, nch),
        out_shape=jax.ShapeDtypeStruct((n, 2, nch + 1, pieces, local_ch, x_cells), BF16),
        in_specs=[pl.BlockSpec(memory_space=pltpu.VMEM)] * 2,
        out_specs=pl.BlockSpec(memory_space=pltpu.VMEM),
        scratch_shapes=[
            pltpu.SemaphoreType.DMA((2,)),
            pltpu.SemaphoreType.DMA((2, n, 2)),
            pltpu.SemaphoreType.DMA((2, n, 2)),
            pltpu.SemaphoreType.DMA((n, nch)),
            pltpu.SemaphoreType.DMA((n, nch)),
            pltpu.SemaphoreType.DMA((n, nch + 1)),
            pltpu.SemaphoreType.DMA((n, nch + 1)),
        ],
        compiler_params=pltpu.CompilerParams(
            collective_id=0, has_side_effects=True, vmem_limit_bytes=LIMIT
        ),
        name="gather_fields",
    )(mine_a, mine_t)


def local_kernel(n, nch, yl, scale, place, buf, w_ref, near, turn, f_ref, g_ref, wg_ref, ext, rolled, ax, tx):
    local_ch = w_ref.shape[1]
    amount = w_ref.shape[2]
    x_cells = buf.shape[-1]
    row = 2 * x_cells
    q = place[0]
    ny = n * yl
    plane = (ny + 2) * row
    flat = ny * row

    for r in range(yl + 2):
        if r == 0:
            source, y, side = lax.rem(q + n - 1, n), yl - 1, 0
        elif r == yl + 1:
            source, y, side = lax.rem(q + 1, n), 0, 2
        else:
            source, y, side = q, r - 1, 1
        for z in range(2):
            at = (z * (yl + 2) + r) * x_cells
            for field, out, size in ((0, ax, amount), (1, tx, local_ch)):
                halves = [
                    buf[source, k, :nch, z * yl + y].reshape(amount, x_cells)
                    if field == 0
                    else buf[source, k, nch, z * yl + y]
                    for k in range(2)
                ]
                for c in range(3):
                    moved = jnp.dot(
                        halves[0], near[side, c, :x_cells], preferred_element_type=F32
                    ) + jnp.dot(halves[1], near[side, c, x_cells:], preferred_element_type=F32)
                    out[c, :, at : at + x_cells] = moved.astype(BF16)

    width = yl * x_cells
    span = (yl + 2) * x_cells
    valid = [(a, z, z + a - 1) for a in range(3) for z in range(2) if 0 <= z + a - 1 < 2]

    def features_step(b, carry):
        out = list(carry)
        for a, z, zz in valid:
            for c in range(3):
                window = ax[c, :, pl.ds(pl.multiple_of(zz * span + b * x_cells, x_cells), width)]
                out[z] += jnp.dot(w_ref[9 * a + 3 * b + c], window, preferred_element_type=F32)
        return tuple(out)

    planes = lax.fori_loop(0, 3, features_step, (jnp.zeros((local_ch, width), F32),) * 2)
    for z in range(2):
        f_ref[:, z * width : (z + 1) * width] = planes[z].astype(BF16)

    def grad_step(b, carry):
        out = list(carry)
        for a, z, _ in valid:
            for c in range(3):
                zz = z + a - 1
                window = tx[c, :, pl.ds(pl.multiple_of(zz * span + b * x_cells, x_cells), width)]
                out[z] += lax.dot_general(
                    w_ref[9 * (2 - a) + 3 * (2 - b) + 2 - c],
                    window,
                    (((0,), (0,)), ((), ())),
                    preferred_element_type=F32,
                )
        return tuple(out)

    planes = lax.fori_loop(0, 3, grad_step, (jnp.zeros((amount, width), F32),) * 2)
    for z in range(2):
        g_ref[:, z * width : (z + 1) * width] = planes[z]

    @pl.loop(0, n)
    def _(source):
        for z in range(2):
            for y in range(yl):
                at = pl.multiple_of(z * plane + (1 + source * yl + y) * row, row)
                to = pl.multiple_of(z * flat + (source * yl + y) * row, row)
                for k in range(2):
                    ext[:, pl.ds(at + k * x_cells, x_cells)] = buf[source, k, :nch, z * yl + y].reshape(
                        amount, x_cells
                    )
                    rolled[1, :, pl.ds(to + k * x_cells, x_cells)] = buf[source, k, nch, z * yl + y]
                line = rolled[1, :, pl.ds(to, row)]
                for c in (0, 2):
                    rolled[c, :, pl.ds(to, row)] = jnp.dot(
                        line, turn[c], preferred_element_type=F32
                    ).astype(BF16)

    for z in range(2):
        first = ext[:, z * plane + row : z * plane + 2 * row]
        last = ext[:, z * plane + ny * row : z * plane + (ny + 1) * row]
        ext[:, z * plane : z * plane + row] = jnp.dot(
            last, turn[3], preferred_element_type=F32
        ).astype(BF16)
        ext[:, z * plane + (ny + 1) * row : (z + 1) * plane] = jnp.dot(
            first, turn[4], preferred_element_type=F32
        ).astype(BF16)

    def weight_step(b, carry):
        for a in range(3):
            total = None
            for a_of, z, zz in valid:
                if a_of != a:
                    continue
                left = rolled[:, :, z * flat : (z + 1) * flat].reshape(3 * local_ch, flat)
                right = ext[:, pl.ds(pl.multiple_of(zz * plane + b * row, row), flat)]
                part = lax.dot_general(
                    left, right, (((1,), (1,)), ((), ())), preferred_element_type=F32
                )
                total = part if total is None else total + part
            wg_ref[pl.ds(9 * a + 3 * b, 3)] = (total * scale).reshape(3, local_ch, amount)
        return carry

    lax.fori_loop(0, 3, weight_step, 0)


def shift_matrix(full, offset, begin, count):
    source = (lax.broadcasted_iota(jnp.int32, (full, count), 1) + begin + offset) % full
    return (lax.broadcasted_iota(jnp.int32, (full, count), 0) == source).astype(BF16)


def on_device(activations, weight, cotangent, shear_shift):
    local_ch, planes, yl, x_cells = activations.shape
    n = lax.axis_size("gy")
    nch = lax.axis_size("ch")
    amount = weight.shape[2]
    full = 2 * x_cells
    q = lax.axis_index("gy")
    shift = shear_shift[0]
    scale = float(planes * yl * n * full) ** (-0.5)

    mine_a = activations.reshape(local_ch, planes * yl, x_cells).transpose(1, 0, 2)
    mine_t = cotangent.reshape(local_ch, planes * yl, x_cells).transpose(1, 0, 2)
    buf = gather(n, nch, mine_a, mine_t)

    begin = lax.axis_index("gx") * x_cells
    below = jnp.where(q == 0, -shift, 0)
    above = jnp.where(q == n - 1, shift, 0)
    near = jnp.stack(
        [
            jnp.stack([shift_matrix(full, ghost + c - 1, begin, x_cells) for c in range(3)])
            for ghost in (below, 0, above)
        ]
    )
    turn = jnp.stack([shift_matrix(full, offset, 0, full) for offset in (1, 0, -1, -shift, shift)])
    ny = n * yl
    vmem = pl.BlockSpec(memory_space=pltpu.VMEM)
    features, term, weight_grad = pl.pallas_call(
        functools.partial(local_kernel, n, nch, yl, scale),
        out_shape=(
            jax.ShapeDtypeStruct((local_ch, planes * yl * x_cells), BF16),
            jax.ShapeDtypeStruct((amount, planes * yl * x_cells), F32),
            jax.ShapeDtypeStruct((27, local_ch, amount), F32),
        ),
        in_specs=[pl.BlockSpec(memory_space=pltpu.SMEM), vmem, vmem, vmem, vmem],
        out_specs=(vmem, vmem, vmem),
        scratch_shapes=[
            pltpu.VMEM((amount, planes * (ny + 2) * full), BF16),
            pltpu.VMEM((3, local_ch, planes * ny * full), BF16),
            pltpu.VMEM((3, amount, planes * (yl + 2) * x_cells), BF16),
            pltpu.VMEM((3, local_ch, planes * (yl + 2) * x_cells), BF16),
        ],
        compiler_params=pltpu.CompilerParams(vmem_limit_bytes=LIMIT),
        name="local_sums",
    )(q.astype(jnp.int32).reshape(1), buf, weight, near, turn)
    grad_in = lax.psum_scatter(term, "ch", scatter_dimension=0, tiled=True)
    shape = (local_ch, planes, yl, x_cells)
    return (features.reshape(shape), grad_in.astype(BF16).reshape(shape), weight_grad)


def solution(mesh):
    return jax.shard_map(
        on_device,
        mesh=mesh,
        in_specs=(
            P("ch", "grp", "gy", "gx"),
            P(None, "ch", None),
            P("ch", "grp", "gy", "gx"),
            P("grp"),
        ),
        out_specs=(P("ch", "grp", "gy", "gx"), P("ch", "grp", "gy", "gx"), P("grp", "ch", None)),
        check_vma=False,
    )
```

time: 471 us -> 116 us (0.25)
  waiting for transfers between devices: 204 us -> 14.5 us
  local copies, waits for them, and re-layouts: 168 us -> 5.64 us
  Pallas kernels: 0 us -> 76.7 us
  matrix products: 24.7 us -> 0 us
  blocking collectives: 22.7 us -> 0 us
  other arithmetic: 25.9 us -> 3.7 us
  starting transfers between devices: 5.81 us -> 0.04 us
    psum x1 -> x0, waiting for transfers between devices: 149 us -> none  [on_device(): grad_sum = lax.psum(grad_acc, ('gy', 'gx'))]
    pallas_call x0 -> x2, Pallas kernels: none -> 76.7 us  [the longest x1 42.8 us: gather(): pl.pallas_call(functools.partial(gather_kernel, n, nch), out_shape=jax.Sh...]
    another operation x56 -> x0, local copies, waits for them, and re-layouts: 67.1 us -> none  [columns(): return jnp.stack(stacked).reshape(27 * extended.shape[0], -1)]
    unnamed x155 -> x2, local copies, waits for them, and re-layouts: 54.7 us -> 3.26 us
    all_gather x2 -> x0, waiting for transfers between devices: 37.9 us -> none  [the longest x1 31.4 us: on_device(): panel = lax.all_gather(input_ext, 'ch', axis=0, tiled=True)]
    slice x8 -> x0, local copies, waits for them, and re-layouts: 32.7 us -> none  [the longest x4 26.2 us: columns(): extended[:, z_from:z_from + planes, y_from:y_from + y_cells, x_from:x_fro...]
    dot_general x3 -> x0, matrix products: 24.7 us -> none  [the longest x1 11 us: on_device(): lax.dot_general(cotan_flat, cols, (((1,), (1,)), ((), ())), preferred_ele...]
    unnamed x1 -> x0, blocking collectives: 22.7 us -> none
  transfers between devices with their start and end apart: 5 -> 1, of which waited for: 5 -> 1; matrix products, arithmetic and copies ran while one was open for 8% -> 1% of each run, Pallas kernels for 0% -> 0%
where the time goes in v1:
time: 116 us
  Pallas kernels  76.7 us (66%)
  between operations  14.9 us (13%)
  waiting for transfers between devices  14.5 us (12%)
  local copies, waits for them, and re-layouts  5.64 us (5%)
  other arithmetic  3.7 us (3%)
    pallas_call x1, Pallas kernels, gather(): pl.pallas_call(functools.partial(gather_kernel, n, nch), out_shape=jax.Sh...  42.8 us
    pallas_call x1, Pallas kernels, on_device(): pl.pallas_call(functools.partial(local_kernel, n, nch, yl, scale), out_sh...  33.9 us
    reduce_scatter x1, waiting for transfers between devices, on_device(): grad_in = lax.psum_scatter(term, 'ch', scatter_dimension=0, tiled=True)  14.5 us
    unnamed x2, local copies, waits for them, and re-layouts  3.26 us
  transfers between devices with their start and end apart: 1, of which 1 were waited for; matrix products, arithmetic and copies ran while one was open for 1% of the time, Pallas kernels for 0%

profile of v1, /device:TPU:0, one launch (start us, length us, event | category | flops | bytes accessed | tf_op | source)
XLA Modules:
  0.0 115.5 jit_solution(13273138897893203747)
XLA Ops:
  7.2 0.0 reduce-scatter.2.cloned.1.call-start
  8.2 1.6 %copy.7 = bf16[192,2,2,128]{3,0,2,1:T(8,128)(2,1)} copy(bf16[192,2,2,128]{3,2,1,0:T(2,128)(2,1)} %param.4) | data formatting | bytes 393216 | tf_op args[0]
  9.9 1.6 %copy.8 = bf16[192,2,2,128]{3,0,2,1:T(8,128)(2,1)} copy(bf16[192,2,2,128]{3,2,1,0:T(2,128)(2,1)} %param.6) | data formatting | bytes 393216 | tf_op args[2]
  11.5 0.1 fusion.1
  11.6 0.1 fusion.2
  11.7 0.1 fusion.3
  11.7 0.1 fusion.4
  11.8 1.0 stack.57.turn
  12.9 42.8 %gather_fields.1.buf = bf16[4,2,3,4,192,128]{5,4,3,2,1,0:T(8,128)(2,1)} custom-call(bf16[4,192,128]{2,1,0:T(8,128)(2,1)} %bitcast.18, bf16[4,192,128]{2,1,0:T(8,128)(2,1)} %bitcast.19), custom_call_target="tpu_custom_call" | custom-call | tf_op jit(solution)/shard_map/gather_fields/pallas_call | solution.py:172
  55.9 1.0 add_convert_fusion.near
  56.9 33.9 %local_sums.1 = (bf16[192,512]{1,0:T(8,128)(2,1)}, f32[384,512]{1,0:T(8,128)}, f32[27,192,384]{2,1,0:T(8,128)}) custom-call(s32[1]{0:T(128)} %bitcast.place, bf16[4,2,3,4,192,128]{5,4,3,2,1,0:T(8,128)(2,1)} %gather_fields.1.buf, bf16[27,192,384]{2,1,0:T(8,128)(2,1)} %w_ref.1, bf16[3,3,256,128]{3,2,1,0:T(8,128)(2,1)} %add_convert_fusion.near, ...), custom_call_target="tpu_custom_call" | custom-call | tf_op jit(solution)/shard_map/local_sums/pallas_call | solution.py:335
  90.7 0.0 reduce-scatter.2.cloned.1.call-update
  90.8 1.7 %reshape.1071 = bf16[192,2,2,128]{3,2,1,0:T(2,128)(2,1)} reshape(bf16[192,512]{1,0:T(8,128)(2,1)} %get-tuple-element.6) | data formatting | bytes 393216 | tf_op jit(solution)/shard_map/reshape | solution.py:355
  92.4 14.5 %reduce-scatter.2.cloned.1.call-done = f32[192,512]{1,0:T(8,128)} async-done(((f32[384,512]{1,0:T(8,128)}), f32[192,512]{1,0:T(8,128)}) %reduce-scatter.2.cloned.1.call-update) | async-done | bytes 393232 | tf_op jit(solution)/shard_map/reduce_scatter | solution.py:353
  107.0 1.0 convert_element_type.115
  108.0 0.7 reshape.1072
  (37 shorter events, 0.5 us)
Async XLA Ops:
  7.2 99.8 %reduce-scatter.2.cloned.1.call-start = ((), (), s32[]{:S(2)}) async-start(), calls=%async_computation.1 | async-start | bytes 1179648 | tf_op jit(solution)/shard_map/reduce_scatter | solution.py:353
Sparse Core Ops, SparseCore 0:
  90.9 16.0 reduce-scatter.1

commit v2 on v0

v2 whole, which is shorter than its diff:
```python
import functools

import jax
import jax.numpy as jnp
from jax import lax
from jax.experimental import pallas as pl
from jax.experimental.pallas import tpu as pltpu
from jax.sharding import PartitionSpec as P

BF16 = jnp.bfloat16
F32 = jnp.float32
LIMIT = 56 * 1024 * 1024

MESH = pl.DeviceIdType.MESH


def layer_kernel(
    n, nch, yl, scale,
    a_ref, t_ref, w_ref, near, turn,
    f_ref, g_ref, wg_ref,
    buf, ext, rolled, ax, tx, term, arrived,
    loc_sem, zs_sem, zr_sem, hs_sem, hr_sem, xs_sem, xr_sem, cs_sem, cr_sem, gs_sem, gr_sem,
):
    q = lax.axis_index("gy")
    h = lax.axis_index("ch")
    c = lax.axis_index("gx")
    other = 1 - c
    local_ch = w_ref.shape[1]
    amount = w_ref.shape[2]
    x_cells = buf.shape[-1]
    row = 2 * x_cells
    ny = n * yl
    plane = (ny + 2) * row
    flat = ny * row
    width = yl * x_cells
    span = (yl + 2) * x_cells
    valid = [(a, z, z + a - 1) for a in range(3) for z in range(2) if 0 <= z + a - 1 < 2]

    whole = (0, 2 * yl)
    halo = {"bottom": (2 * yl - 2, 2), "top": (0, 2)}
    rest = {"bottom": (0, 2 * yl - 2), "top": (2, 2 * yl - 2)}
    ends = {"bottom": (q == 0, n - 1), "top": (q == n - 1, 0)}

    def copy(slot, to, send, recv):
        return pltpu.make_async_remote_copy(
            src_ref=slot, dst_ref=slot, send_sem=send, recv_sem=recv, device_id=to, device_id_type=MESH
        )

    def channel(kind):
        return h if kind == 0 else nch

    def z_copy(step, direction, kind, source, part=whole):
        return copy(
            buf.at[source, c, channel(kind), pl.ds(*part)],
            {"gy": q - 1 if direction == 0 else q + 1},
            zs_sem.at[direction, step, kind],
            zr_sem.at[direction, step, kind],
        )

    def h_copy(kind, source, part, to):
        return copy(
            buf.at[source, c, channel(kind), pl.ds(*part)], {"gy": to}, hs_sem.at[kind], hr_sem.at[kind]
        )

    def x_copy(source, d, part=whole, sub=0, arrival=False):
        panel = lax.rem(h - d + nch, nch) if arrival else h
        return copy(
            buf.at[source, c, panel, pl.ds(*part)],
            {"ch": lax.rem(h + d, nch)},
            xs_sem.at[source, d, sub],
            xr_sem.at[source, d, sub],
        )

    def c_copy(source, d, part=whole, sub=0, side=None):
        kind = nch if d == nch else lax.rem(h - d + nch, nch)
        return copy(
            buf.at[source, c if side is None else side, kind, pl.ds(*part)],
            {"gx": other},
            cs_sem.at[source, d, sub],
            cr_sem.at[source, d, sub],
        )

    def pass_on(source, kind, part=whole, sub=0):
        if kind == 0:
            for d in range(1, nch):
                x_copy(source, d, part, sub).start()
            c_copy(source, 0, part, sub).start()
        else:
            c_copy(source, nch, part, sub).start()

    def relay(source, part=whole, sub=0):
        for d in range(1, nch):
            x_copy(source, d, part, sub, True).wait_recv()
            c_copy(source, d, part, sub).start()

    def from_core(source, kinds, part=whole, sub=0):
        for d in kinds:
            c_copy(source, d, part, sub, other).wait_recv()

    fields = range(nch)

    def each(step, body):
        if step < n - 1:

            @pl.when(q + step < n)
            def _():
                body(0, q + step, whole)

            @pl.when(q - step >= 0)
            def _():
                body(1, q - step, whole)
        else:
            for direction, name in ((0, "bottom"), (1, "top")):

                @pl.when(ends[name][0])
                def _(direction=direction, name=name):
                    body(direction, ends[name][1], rest[name])

    def onward(step, direction, kind, source):
        def go(part):
            z_copy(step, direction, kind, source, part).start()

        last = step == n - 2
        if direction == 0:

            @pl.when(q >= 1)
            def _():
                go(rest["bottom"] if last else whole)
        else:

            @pl.when(q < n - 1)
            def _():
                go(rest["top"] if last else whole)

    barrier = pltpu.get_barrier_semaphore()

    def greet(to):
        pl.semaphore_signal(barrier, inc=1, device_id=to, device_id_type=MESH)

    @pl.when(q > 0)
    def _():
        greet({"gy": q - 1})

    @pl.when(q < n - 1)
    def _():
        greet({"gy": q + 1})

    for name in ("bottom", "top"):

        @pl.when(ends[name][0])
        def _(name=name):
            greet({"gy": ends[name][1]})

    for d in range(1, nch):
        greet({"ch": lax.rem(h + d, nch)})
    greet({"gx": other})
    own_a = pltpu.make_async_copy(a_ref, buf.at[q, c, h], loc_sem.at[0])
    own_t = pltpu.make_async_copy(t_ref, buf.at[q, c, nch], loc_sem.at[1])
    own_a.start()
    own_t.start()
    own_a.wait()
    own_t.wait()
    pl.semaphore_wait(barrier, 2 + nch)

    for kind in (1, 0):

        @pl.when(q == 0)
        def _(kind=kind):
            h_copy(kind, 0, halo["top"], n - 1).start()

        @pl.when(q == n - 1)
        def _(kind=kind):
            h_copy(kind, n - 1, halo["bottom"], 0).start()

    for kind in range(2):
        for direction in range(2):
            onward(0, direction, kind, q)
        pass_on(q, kind)

    def take(step):
        for kind in range(2):

            def body(direction, source, part, kind=kind):
                z_copy(step - 1, direction, kind, source, part).wait_recv()
                if step < n - 1:
                    onward(step, direction, kind, source)
                pass_on(source, kind, part)

            each(step, body)

    take(1)
    for name in ("bottom", "top"):

        @pl.when(ends[name][0])
        def _(name=name):
            source, part = ends[name][1], halo[name]
            for kind in (1, 0):
                h_copy(kind, source, part, source).wait_recv()
                pass_on(source, kind, part, 1)

    relay(q)

    from_core(q, (nch,))
    each(1, lambda direction, source, part: from_core(source, (nch,), part))
    for name in ("bottom", "top"):

        @pl.when(ends[name][0])
        def _(name=name):
            from_core(ends[name][1], (nch,), halo[name], 1)

    def surround(field):
        out = ax if field == 0 else tx
        for r in range(yl + 2):
            if r == 0:
                source, y, side = lax.rem(q + n - 1, n), yl - 1, 0
            elif r == yl + 1:
                source, y, side = lax.rem(q + 1, n), 0, 2
            else:
                source, y, side = q, r - 1, 1
            for z in range(2):
                at = (z * (yl + 2) + r) * x_cells
                halves = [
                    buf[source, k, :nch, 2 * y + z].reshape(amount, x_cells)
                    if field == 0
                    else buf[source, k, nch, 2 * y + z]
                    for k in range(2)
                ]
                for s in range(3):
                    moved = jnp.dot(
                        halves[0], near[side, s, :x_cells], preferred_element_type=F32
                    ) + jnp.dot(halves[1], near[side, s, x_cells:], preferred_element_type=F32)
                    out[s, :, at : at + x_cells] = moved.astype(BF16)

    surround(1)

    def grad_step(b, carry):
        out = list(carry)
        for a, z, zz in valid:
            for s in range(3):
                window = tx[s, :, pl.ds(pl.multiple_of(zz * span + b * x_cells, x_cells), width)]
                out[z] += lax.dot_general(
                    w_ref[9 * (2 - a) + 3 * (2 - b) + 2 - s],
                    window,
                    (((0,), (0,)), ((), ())),
                    preferred_element_type=F32,
                )
        return tuple(out)

    planes = lax.fori_loop(0, 3, grad_step, (jnp.zeros((amount, width), F32),) * 2)
    for z in range(2):
        term[:, :, z * width : (z + 1) * width] = planes[z].reshape(nch, local_ch, width)

    each(1, lambda direction, source, part: relay(source, part))
    for name in ("bottom", "top"):

        @pl.when(ends[name][0])
        def _(name=name):
            relay(ends[name][1], halo[name], 1)

    def g_copy(d):
        to = lax.rem(h + d, nch)
        return pltpu.make_async_remote_copy(
            src_ref=term.at[to],
            dst_ref=arrived.at[d],
            send_sem=gs_sem.at[d],
            recv_sem=gr_sem.at[d],
            device_id={"ch": to},
            device_id_type=MESH,
        )

    for step in range(2, n - 1):
        take(step)
        if step == 2:
            for d in range(1, nch):
                g_copy(d).start()
        if step > 2:
            each(step - 1, lambda direction, source, part: relay(source, part))

    from_core(q, fields)
    each(1, lambda direction, source, part: from_core(source, fields, part))
    for name in ("bottom", "top"):

        @pl.when(ends[name][0])
        def _(name=name):
            from_core(ends[name][1], fields, halo[name], 1)

    surround(0)

    def features_step(b, carry):
        out = list(carry)
        for a, z, zz in valid:
            for s in range(3):
                window = ax[s, :, pl.ds(pl.multiple_of(zz * span + b * x_cells, x_cells), width)]
                out[z] += jnp.dot(w_ref[9 * a + 3 * b + s], window, preferred_element_type=F32)
        return tuple(out)

    planes = lax.fori_loop(0, 3, features_step, (jnp.zeros((local_ch, width), F32),) * 2)
    for z in range(2):
        f_ref[:, z * width : (z + 1) * width] = planes[z].astype(BF16)

    if n > 3:
        each(n - 2, lambda direction, source, part: relay(source, part))
    for step in range(2, n - 1):
        each(
            step, lambda direction, source, part: from_core(source, range(nch + 1), part)
        )

    late = jnp.where(2 * q < n, n - 1, 0)
    base = jnp.where(2 * q < n, 0, 1)

    def lay_out(source):
        for z in range(2):
            for y in range(yl):
                at = pl.multiple_of(z * plane + (1 + source * yl + y) * row, row)
                to = pl.multiple_of(z * flat + (source * yl + y) * row, row)
                for k in range(2):
                    ext[:, pl.ds(at + k * x_cells, x_cells)] = buf[source, k, :nch, 2 * y + z].reshape(
                        amount, x_cells
                    )
                    rolled[1, :, pl.ds(to + k * x_cells, x_cells)] = buf[source, k, nch, 2 * y + z]
                line = rolled[1, :, pl.ds(to, row)]
                for s in (0, 2):
                    rolled[s, :, pl.ds(to, row)] = jnp.dot(
                        line, turn[s], preferred_element_type=F32
                    ).astype(BF16)

    @pl.loop(0, n - 1)
    def _(k):
        lay_out(base + k)

    def products(a, b, start, rows):
        total = None
        for a_of, z, zz in valid:
            if a_of != a:
                continue
            left = rolled[:, :, pl.ds(pl.multiple_of(z * flat + start * row, row), rows * row)]
            right = ext[:, pl.ds(pl.multiple_of(zz * plane + (start + b) * row, row), rows * row)]
            part = lax.dot_general(
                left.reshape(3 * local_ch, rows * row),
                right,
                (((1,), (1,)), ((), ())),
                preferred_element_type=F32,
            )
            total = part if total is None else total + part
        return (total * scale).reshape(3, local_ch, amount)

    def early(a):
        many = (n - 1) * yl
        first = base * yl
        for b in range(3):
            at = 9 * a + 3 * b
            if b == 1:
                wg_ref[at : at + 3] = products(a, b, first, many)
            else:
                wg_ref[at : at + 3] = products(a, b, first + (1 if b == 0 else 0), many - 1)

    early(0)
    early(2)
    take(n - 1)
    early(1)
    each(n - 1, lambda direction, source, part: relay(source, part))
    for d in range(1, nch):
        g_copy(d).wait_recv()
    total = term[h]
    for d in range(1, nch):
        total = total + arrived[d]
    g_ref[...] = total.astype(BF16)
    each(n - 1, lambda direction, source, part: from_core(source, range(nch + 1), part))

    lay_out(late)
    for z in range(2):
        first = ext[:, z * plane + row : z * plane + 2 * row]
        last = ext[:, z * plane + ny * row : z * plane + (ny + 1) * row]
        ext[:, z * plane : z * plane + row] = jnp.dot(
            last, turn[3], preferred_element_type=F32
        ).astype(BF16)
        ext[:, z * plane + (ny + 1) * row : (z + 1) * plane] = jnp.dot(
            first, turn[4], preferred_element_type=F32
        ).astype(BF16)

    for a in range(3):
        for b in range(3):
            at = 9 * a + 3 * b
            more = products(a, b, late * yl, yl)
            if b == 0:
                more = more + products(a, b, lax.rem(late * yl + yl, ny), 1)
            if b == 2:
                more = more + products(a, b, lax.rem(late * yl + ny - 1, ny), 1)
            wg_ref[at : at + 3] += more

    for step in range(n - 1):
        for kind in range(2):
            last = step == n - 2

            @pl.when((q >= 1) & (q + step < n))
            def _():
                z_copy(step, 0, kind, q + step, rest["bottom"] if last else whole).wait_send()

            @pl.when((q < n - 1) & (q - step >= 0))
            def _():
                z_copy(step, 1, kind, q - step, rest["top"] if last else whole).wait_send()

    def gone(source, part=whole, sub=0):
        for d in range(1, nch):
            x_copy(source, d, part, sub).wait_send()
        for d in range(nch + 1):
            c_copy(source, d, part, sub).wait_send()

    gone(q)
    for step in range(1, n):
        each(step, lambda direction, source, part: gone(source, part))
    for name, mine in (("bottom", "top"), ("top", "bottom")):

        @pl.when(ends[name][0])
        def _(name=name, mine=mine):
            gone(ends[name][1], halo[name], 1)
            for kind in range(2):
                h_copy(kind, q, halo[mine], ends[name][1]).wait_send()

    for d in range(1, nch):
        g_copy(d).wait_send()


def shift_matrix(full, offset, begin, count):
    source = (lax.broadcasted_iota(jnp.int32, (full, count), 1) + begin + offset) % full
    return (lax.broadcasted_iota(jnp.int32, (full, count), 0) == source).astype(BF16)


def on_device(activations, weight, cotangent, shear_shift):
    local_ch, planes, yl, x_cells = activations.shape
    n = lax.axis_size("gy")
    nch = lax.axis_size("ch")
    amount = weight.shape[2]
    full = 2 * x_cells
    ny = n * yl
    q = lax.axis_index("gy")
    shift = shear_shift[0]
    scale = float(planes * ny * full) ** (-0.5)

    def pieces(field):
        return field.transpose(2, 1, 0, 3).reshape(planes * yl, local_ch, x_cells)

    begin = lax.axis_index("gx") * x_cells
    below = jnp.where(q == 0, -shift, 0)
    above = jnp.where(q == n - 1, shift, 0)
    near = jnp.stack(
        [
            jnp.stack([shift_matrix(full, ghost + c - 1, begin, x_cells) for c in range(3)])
            for ghost in (below, 0, above)
        ]
    )
    turn = jnp.stack([shift_matrix(full, offset, 0, full) for offset in (1, 0, -1, -shift, shift)])
    vmem = pl.BlockSpec(memory_space=pltpu.VMEM)
    cells = planes * yl * x_cells
    dma = pltpu.SemaphoreType.DMA
    features, grad_in, weight_grad = pl.pallas_call(
        functools.partial(layer_kernel, n, nch, yl, scale),
        out_shape=(
            jax.ShapeDtypeStruct((local_ch, cells), BF16),
            jax.ShapeDtypeStruct((local_ch, cells), BF16),
            jax.ShapeDtypeStruct((27, local_ch, amount), F32),
        ),
        in_specs=[vmem] * 5,
        out_specs=(vmem,) * 3,
        scratch_shapes=[
            pltpu.VMEM((n, 2, nch + 1, planes * yl, local_ch, x_cells), BF16),
            pltpu.VMEM((amount, planes * (ny + 2) * full), BF16),
            pltpu.VMEM((3, local_ch, planes * ny * full), BF16),
            pltpu.VMEM((3, amount, planes * (yl + 2) * x_cells), BF16),
            pltpu.VMEM((3, local_ch, planes * (yl + 2) * x_cells), BF16),
            pltpu.VMEM((nch, local_ch, cells), F32),
            pltpu.VMEM((nch, local_ch, cells), F32),
            dma((2,)),
            dma((2, n, 2)),
            dma((2, n, 2)),
            dma((2,)),
            dma((2,)),
            dma((n, nch, 2)),
            dma((n, nch, 2)),
            dma((n, nch + 1, 2)),
            dma((n, nch + 1, 2)),
            dma((nch,)),
            dma((nch,)),
        ],
        compiler_params=pltpu.CompilerParams(
            collective_id=0, has_side_effects=True, vmem_limit_bytes=LIMIT
        ),
        name="layer",
    )(pieces(activations), pieces(cotangent), weight, near, turn)
    shape = (local_ch, planes, yl, x_cells)
    return (features.reshape(shape), grad_in.reshape(shape), weight_grad)


def solution(mesh):
    return jax.shard_map(
        on_device,
        mesh=mesh,
        in_specs=(
            P("ch", "grp", "gy", "gx"),
            P(None, "ch", None),
            P("ch", "grp", "gy", "gx"),
            P("grp"),
        ),
        out_specs=(P("ch", "grp", "gy", "gx"), P("ch", "grp", "gy", "gx"), P("grp", "ch", None)),
        check_vma=False,
    )
```

time: 471 us -> 76.9 us (0.16)
  waiting for transfers between devices: 204 us -> 0 us
  local copies, waits for them, and re-layouts: 168 us -> 13.9 us
  Pallas kernels: 0 us -> 58.2 us
  matrix products: 24.7 us -> 0 us
  other arithmetic: 25.9 us -> 2.71 us
  blocking collectives: 22.7 us -> 0 us
  between operations: 15.8 us -> 1.53 us
  starting transfers between devices: 5.81 us -> 0 us
    psum x1 -> x0, waiting for transfers between devices: 149 us -> none  [on_device(): grad_sum = lax.psum(grad_acc, ('gy', 'gx'))]
    another operation x56 -> x0, local copies, waits for them, and re-layouts: 67.1 us -> none  [columns(): return jnp.stack(stacked).reshape(27 * extended.shape[0], -1)]
    pallas_call x0 -> x1, Pallas kernels: none -> 58.2 us  [on_device(): pl.pallas_call(functools.partial(layer_kernel, n, nch, yl, scale), out_sh...]
    unnamed x155 -> x1, local copies, waits for them, and re-layouts: 54.7 us -> 7.36 us
    all_gather x2 -> x0, waiting for transfers between devices: 37.9 us -> none  [the longest x1 31.4 us: on_device(): panel = lax.all_gather(input_ext, 'ch', axis=0, tiled=True)]
    slice x8 -> x0, local copies, waits for them, and re-layouts: 32.7 us -> none  [the longest x4 26.2 us: columns(): extended[:, z_from:z_from + planes, y_from:y_from + y_cells, x_from:x_fro...]
    dot_general x3 -> x0, matrix products: 24.7 us -> none  [the longest x1 11 us: on_device(): lax.dot_general(cotan_flat, cols, (((1,), (1,)), ((), ())), preferred_ele...]
    unnamed x1 -> x0, blocking collectives: 22.7 us -> none
  transfers between devices with their start and end apart: 5 -> 0, of which waited for: 5 -> 0; matrix products, arithmetic and copies ran while one was open for 8% -> 0% of each run, Pallas kernels for 0% -> 0%
where the time goes in v2:
time: 76.9 us; the launch traced here: 76.4 us
  Pallas kernels  58.2 us (76%)
  local copies, waits for them, and re-layouts  13.9 us (18%)
  other arithmetic  2.71 us (4%)
  between operations  1.53 us (2%)
    pallas_call x1, Pallas kernels, on_device(): pl.pallas_call(functools.partial(layer_kernel, n, nch, yl, scale), out_sh...  58.2 us
    unnamed x1, local copies, waits for them, and re-layouts  7.36 us
    reshape x2, local copies, waits for them, and re-layouts, on_device(): return (features.reshape(shape), grad_in.reshape(shape), weight_grad)  3.31 us
    transpose x2, local copies, waits for them, and re-layouts, pieces(): return field.transpose(2, 1, 0, 3).reshape(planes * yl, local_ch, x_cells)  3.26 us

profile of v2, /device:TPU:0, one launch (start us, length us, event | category | flops | bytes accessed | tf_op | source)
XLA Modules:
  0.0 76.4 jit_solution(13197863933015162472)
XLA Ops:
  2.0 1.6 %copy.7 = bf16[2,2,192,128]{3,2,1,0:T(8,128)(2,1)} copy(bf16[2,2,192,128]{3,0,1,2:T(2,128)(2,1)} %bitcast.17) | data formatting | bytes 393216 | tf_op jit(solution)/shard_map/transpose | solution.py:441
  3.6 1.6 %copy.8 = bf16[2,2,192,128]{3,2,1,0:T(8,128)(2,1)} copy(bf16[2,2,192,128]{3,0,1,2:T(2,128)(2,1)} %bitcast.18) | data formatting | bytes 393216 | tf_op jit(solution)/shard_map/transpose | solution.py:441
  5.3 1.0 %add_convert_fusion.near = bf16[3,3,256,128]{3,2,1,0:T(8,128)(2,1)} fusion(pred[1,3,256,128]{3,2,1,0:T(8,128)(4,1)S(1)} %add_bitcast_fusion.2, pred[1,3,256,128]{3,2,1,0:T(8,128)(4,1)S(1)} %add_bitcast_fusion.1, pred[1,3,256,128]{3,2,1,0:T(8,128)(4,1)S(1)} %add_bitcast_fusion), kind=kLoop, calls=%fused_computation | loop fusion | flops 884736 | bytes 884736 | tf_op jit(solution)/shard_map/stack | solution.py:446
  6.3 0.1 fusion.1
  6.4 0.1 fusion.2
  6.4 0.1 fusion.3
  6.5 0.1 fusion.4
  6.5 1.0 %stack.57.turn = bf16[5,256,256]{2,1,0:T(8,128)(2,1)} convert(pred[5,256,256]{2,1,0:T(8,128)(4,1)S(1)} %fusion.4) | non-fusion elementwise | flops 327680 | bytes 983040 | tf_op jit(solution)/shard_map/stack | solution.py:452
  7.5 58.2 %layer.1 = (bf16[192,512]{1,0:T(8,128)(2,1)}, bf16[192,512]{1,0:T(8,128)(2,1)}, f32[27,192,384]{2,1,0:T(8,128)}) custom-call(bf16[4,192,128]{2,1,0:T(8,128)(2,1)} %bitcast.15, bf16[4,192,128]{2,1,0:T(8,128)(2,1)} %bitcast.16, bf16[27,192,384]{2,1,0:T(8,128)(2,1)} %w_ref.1, bf16[3,3,256,128]{3,2,1,0:T(8,128)(2,1)} %add_convert_fusion.near, ...), custom_call_target="tpu_custom_call" | custom-call | tf_op jit(solution)/shard_map/layer/pallas_call | solution.py:456
  65.7 1.7 %reshape.1067 = bf16[192,2,2,128]{3,2,1,0:T(2,128)(2,1)} reshape(bf16[192,512]{1,0:T(8,128)(2,1)} %get-tuple-element.6) | data formatting | bytes 393216 | tf_op jit(solution)/shard_map/reshape | solution.py:491
  67.4 1.7 %reshape.1068 = bf16[192,2,2,128]{3,2,1,0:T(2,128)(2,1)} reshape(bf16[192,512]{1,0:T(8,128)(2,1)} %get-tuple-element.7) | data formatting | bytes 393216 | tf_op jit(solution)/shard_map/reshape | solution.py:491
  69.0 7.4 %copy.15 = f32[27,192,384]{2,1,0:T(8,128)} copy(f32[27,192,384]{2,1,0:T(8,128)} %get-tuple-element.49) | data formatting | bytes 15925248
  (37 shorter events, 0.5 us)

commit v3 on v2

--- a/solution.py
+++ b/solution.py
@@ -9,17 +9,16 @@
 
 BF16 = jnp.bfloat16
 F32 = jnp.float32
-LIMIT = 56 * 1024 * 1024
 
 MESH = pl.DeviceIdType.MESH
 
 
 def layer_kernel(
     n, nch, yl, scale,
-    a_ref, t_ref, w_ref, near, turn,
+    shear_ref, a_ref, t_ref, w_ref,
     f_ref, g_ref, wg_ref,
-    buf, ext, rolled, ax, tx, term, arrived,
-    loc_sem, zs_sem, zr_sem, hs_sem, hr_sem, xs_sem, xr_sem, cs_sem, cr_sem, gs_sem, gr_sem,
+    buf, ext, rolled, ax, tx, term, arrived, near, turn,
+    zs_sem, zr_sem, hs_sem, hr_sem, xs_sem, xr_sem, cs_sem, cr_sem, gs_sem, gr_sem,
 ):
     q = lax.axis_index("gy")
     h = lax.axis_index("ch")
@@ -154,12 +153,11 @@
     for d in range(1, nch):
         greet({"ch": lax.rem(h + d, nch)})
     greet({"gx": other})
-    own_a = pltpu.make_async_copy(a_ref, buf.at[q, c, h], loc_sem.at[0])
-    own_t = pltpu.make_async_copy(t_ref, buf.at[q, c, nch], loc_sem.at[1])
-    own_a.start()
-    own_t.start()
-    own_a.wait()
-    own_t.wait()
+    for field, kind in ((a_ref, h), (t_ref, nch)):
+        for z in range(2):
+            both = field[:, z].astype(F32)
+            for y in range(yl):
+                buf[q, c, kind, 2 * y + z] = both[:, y].astype(BF16)
     pl.semaphore_wait(barrier, 2 + nch)
 
     for kind in (1, 0):
@@ -187,6 +185,20 @@
                 pass_on(source, kind, part)
 
             each(step, body)
+
+    shift = shear_ref[0]
+
+    def shift_matrix(offset, count):
+        source = lax.broadcasted_iota(jnp.int32, (row, count), 1) + lax.rem(offset + 2 * row, row)
+        source = jnp.where(source >= row, source - row, source)
+        found = lax.broadcasted_iota(jnp.int32, (row, count), 0) == source
+        return jnp.where(found, 1.0, 0.0).astype(BF16)
+
+    for side, ghost in enumerate((jnp.where(q == 0, -shift, 0), 0, jnp.where(q == n - 1, shift, 0))):
+        for s in range(3):
+            near[side, s] = shift_matrix(ghost + c * x_cells + s - 1, x_cells)
+    for k, offset in enumerate((1, 0, -1, -shift, shift)):
+        turn[k] = shift_matrix(offset, row)
 
     take(1)
     for name in ("bottom", "top"):
@@ -286,6 +298,9 @@
 
     surround(0)
 
+    def rows_apart(flat_rows):
+        return jnp.stack([flat_rows[:, y * x_cells : (y + 1) * x_cells] for y in range(yl)], axis=1)
+
     def features_step(b, carry):
         out = list(carry)
         for a, z, zz in valid:
@@ -296,7 +311,7 @@
 
     planes = lax.fori_loop(0, 3, features_step, (jnp.zeros((local_ch, width), F32),) * 2)
     for z in range(2):
-        f_ref[:, z * width : (z + 1) * width] = planes[z].astype(BF16)
+        f_ref[:, z] = rows_apart(planes[z]).astype(BF16)
 
     if n > 3:
         each(n - 2, lambda direction, source, part: relay(source, part))
@@ -364,7 +379,8 @@
     total = term[h]
     for d in range(1, nch):
         total = total + arrived[d]
-    g_ref[...] = total.astype(BF16)
+    for z in range(2):
+        g_ref[:, z] = rows_apart(total[:, z * width : (z + 1) * width]).astype(BF16)
     each(n - 1, lambda direction, source, part: from_core(source, range(nch + 1), part))
 
     lay_out(late)
@@ -421,11 +437,6 @@
         g_copy(d).wait_send()
 
 
-def shift_matrix(full, offset, begin, count):
-    source = (lax.broadcasted_iota(jnp.int32, (full, count), 1) + begin + offset) % full
-    return (lax.broadcasted_iota(jnp.int32, (full, count), 0) == source).astype(BF16)
-
-
 def on_device(activations, weight, cotangent, shear_shift):
     local_ch, planes, yl, x_cells = activations.shape
     n = lax.axis_size("gy")
@@ -433,34 +444,24 @@
     amount = weight.shape[2]
     full = 2 * x_cells
     ny = n * yl
-    q = lax.axis_index("gy")
-    shift = shear_shift[0]
     scale = float(planes * ny * full) ** (-0.5)
 
-    def pieces(field):
-        return field.transpose(2, 1, 0, 3).reshape(planes * yl, local_ch, x_cells)
-
-    begin = lax.axis_index("gx") * x_cells
-    below = jnp.where(q == 0, -shift, 0)
-    above = jnp.where(q == n - 1, shift, 0)
-    near = jnp.stack(
-        [
-            jnp.stack([shift_matrix(full, ghost + c - 1, begin, x_cells) for c in range(3)])
-            for ghost in (below, 0, above)
-        ]
-    )
-    turn = jnp.stack([shift_matrix(full, offset, 0, full) for offset in (1, 0, -1, -shift, shift)])
     vmem = pl.BlockSpec(memory_space=pltpu.VMEM)
     cells = planes * yl * x_cells
     dma = pltpu.SemaphoreType.DMA
+    blocks = n * 2 * (nch + 1) * 2 * yl * local_ch * x_cells
+    whole = planes * (ny + 2) * full * (amount + 3 * local_ch)
+    around = 3 * (amount + local_ch) * planes * (yl + 2) * x_cells
+    held = 2 * (blocks + whole + around) + 8 * amount * cells + 27 * local_ch * amount * 6
+    limit = min(held + 14 * 2**20, 60 * 2**20)
     features, grad_in, weight_grad = pl.pallas_call(
         functools.partial(layer_kernel, n, nch, yl, scale),
         out_shape=(
-            jax.ShapeDtypeStruct((local_ch, cells), BF16),
-            jax.ShapeDtypeStruct((local_ch, cells), BF16),
+            jax.ShapeDtypeStruct(activations.shape, BF16),
+            jax.ShapeDtypeStruct(activations.shape, BF16),
             jax.ShapeDtypeStruct((27, local_ch, amount), F32),
         ),
-        in_specs=[vmem] * 5,
+        in_specs=[pl.BlockSpec(memory_space=pltpu.SMEM)] + [vmem] * 3,
         out_specs=(vmem,) * 3,
         scratch_shapes=[
             pltpu.VMEM((n, 2, nch + 1, planes * yl, local_ch, x_cells), BF16),
@@ -470,7 +471,8 @@
             pltpu.VMEM((3, local_ch, planes * (yl + 2) * x_cells), BF16),
             pltpu.VMEM((nch, local_ch, cells), F32),
             pltpu.VMEM((nch, local_ch, cells), F32),
-            dma((2,)),
+            pltpu.VMEM((3, 3, full, x_cells), BF16),
+            pltpu.VMEM((5, full, full), BF16),
             dma((2, n, 2)),
             dma((2, n, 2)),
             dma((2,)),
@@ -483,12 +485,11 @@
             dma((nch,)),
         ],
         compiler_params=pltpu.CompilerParams(
-            collective_id=0, has_side_effects=True, vmem_limit_bytes=LIMIT
+            collective_id=0, has_side_effects=True, vmem_limit_bytes=limit
         ),
         name="layer",
-    )(pieces(activations), pieces(cotangent), weight, near, turn)
-    shape = (local_ch, planes, yl, x_cells)
-    return (features.reshape(shape), grad_in.reshape(shape), weight_grad)
+    )(shear_shift, activations, cotangent, weight)
+    return (features, grad_in, weight_grad)
 
 
 def solution(mesh):

time: 76.9 us -> 70.1 us (0.912)
  other arithmetic: 2.71 us -> 0 us
  Pallas kernels: 58.2 us -> 55.8 us
  local copies, waits for them, and re-layouts: 13.9 us -> 12.7 us
    unnamed x1 -> x9, local copies, waits for them, and re-layouts: 7.36 us -> 12.7 us
    reshape x2 -> x0, local copies, waits for them, and re-layouts: 3.31 us -> none  [on_device(): return (features.reshape(shape), grad_in.reshape(shape), weight_grad)]
    transpose x2 -> x0, local copies, waits for them, and re-layouts: 3.26 us -> none  [pieces(): return field.transpose(2, 1, 0, 3).reshape(planes * yl, local_ch, x_cells)]
    pallas_call x1, Pallas kernels: 58.2 us -> 55.8 us  [on_device(): pl.pallas_call(functools.partial(layer_kernel, n, nch, yl, scale), out_sh...]
    another operation x6 -> x0, other arithmetic: 2.03 us -> none  [the longest x4 1.02 us: on_device(): jnp.stack([jnp.stack([shift_matrix(full, ghost + c - 1, begin, x_cells) f...]
where the time goes in v3:
time: 70.1 us; the launch traced here: 69.8 us
  Pallas kernels  55.8 us (80%)
  local copies, waits for them, and re-layouts  12.7 us (18%)
  between operations  1.3 us (2%)
    pallas_call x1, Pallas kernels, on_device(): pl.pallas_call(functools.partial(layer_kernel, n, nch, yl, scale), out_sh...  55.8 us
    unnamed x9, local copies, waits for them, and re-layouts  12.7 us

profile of v3, /device:TPU:0, one launch (start us, length us, event | category | flops | bytes accessed | tf_op | source)
XLA Modules:
  0.0 69.8 jit_solution(17307697761675703964)
XLA Ops:
  1.3 0.0 copy-start
  1.3 2.1 %copy-done = bf16[27,192,384]{2,1,0:T(8,128)(2,1)S(1)} copy-done((bf16[27,192,384]{2,1,0:T(8,128)(2,1)S(1)}, bf16[27,192,384]{2,1,0:T(8,128)(2,1)}, u32[]{:S(2)}) %copy-start) | copy-done | bytes 3981336
  3.4 0.0 copy-start.1
  3.4 0.9 %copy-done.1 = bf16[192,2,2,128]{3,2,1,0:T(2,128)(2,1)S(1)} copy-done((bf16[192,2,2,128]{3,2,1,0:T(2,128)(2,1)S(1)}, bf16[192,2,2,128]{3,2,1,0:T(2,128)(2,1)}, u32[]{:S(2)}) %copy-start.1) | copy-done | bytes 196632
  4.3 0.0 copy-start.2
  4.3 0.9 %copy-done.2 = bf16[192,2,2,128]{3,2,1,0:T(2,128)(2,1)S(1)} copy-done((bf16[192,2,2,128]{3,2,1,0:T(2,128)(2,1)S(1)}, bf16[192,2,2,128]{3,2,1,0:T(2,128)(2,1)}, u32[]{:S(2)}) %copy-start.2) | copy-done | bytes 196632
  5.3 55.8 %layer.1 = (bf16[192,2,2,128]{3,2,1,0:T(2,128)(2,1)S(1)}, bf16[192,2,2,128]{3,2,1,0:T(2,128)(2,1)S(1)}, f32[27,192,384]{2,1,0:T(8,128)}) custom-call(s32[1]{0:T(128)S(6)} %copy.10.shear_ref, bf16[192,2,2,128]{3,2,1,0:T(2,128)(2,1)S(1)} %copy-done.1, bf16[192,2,2,128]{3,2,1,0:T(2,128)(2,1)S(1)} %copy-done.2, bf16[27,192,384]{2,1,0:T(8,128)(2,1)S(1)} %copy-done), custom_call_target="tpu_custom_call" | custom-call | tf_op jit(solution)/shard_map/layer/pallas_call | solution.py:457
  61.1 0.7 copy.11
  61.8 0.7 copy.12
  62.5 7.4 %copy.13 = f32[27,192,384]{2,1,0:T(8,128)} copy(f32[27,192,384]{2,1,0:T(8,128)} %get-tuple-element.8) | data formatting | bytes 15925248
Async XLA Ops:
  1.3 2.1 %copy-start = (bf16[27,192,384]{2,1,0:T(8,128)(2,1)S(1)}, bf16[27,192,384]{2,1,0:T(8,128)(2,1)}, u32[]{:S(2)}) copy-start(bf16[27,192,384]{2,1,0:T(8,128)(2,1)} %w_ref.1) | copy-start | bytes 11943940
  3.4 0.9 %copy-start.1 = (bf16[192,2,2,128]{3,2,1,0:T(2,128)(2,1)S(1)}, bf16[192,2,2,128]{3,2,1,0:T(2,128)(2,1)}, u32[]{:S(2)}) copy-start(bf16[192,2,2,128]{3,2,1,0:T(2,128)(2,1)} %a_ref.1) | copy-start | bytes 589828
  4.3 0.9 %copy-start.2 = (bf16[192,2,2,128]{3,2,1,0:T(2,128)(2,1)S(1)}, bf16[192,2,2,128]{3,2,1,0:T(2,128)(2,1)}, u32[]{:S(2)}) copy-start(bf16[192,2,2,128]{3,2,1,0:T(2,128)(2,1)} %t_ref.1) | copy-start | bytes 589828

commit v4 on v3

--- a/solution.py
+++ b/solution.py
@@ -453,7 +453,7 @@
     whole = planes * (ny + 2) * full * (amount + 3 * local_ch)
     around = 3 * (amount + local_ch) * planes * (yl + 2) * x_cells
     held = 2 * (blocks + whole + around) + 8 * amount * cells + 27 * local_ch * amount * 6
-    limit = min(held + 14 * 2**20, 60 * 2**20)
+    limit = min(held + 4 * 2**20, 60 * 2**20)
     features, grad_in, weight_grad = pl.pallas_call(
         functools.partial(layer_kernel, n, nch, yl, scale),
         out_shape=(

time: 70.1 us -> 62.9 us (0.90)
  local copies, waits for them, and re-layouts: 12.7 us -> 8.58 us
  Pallas kernels: 55.8 us -> 52.8 us
    unnamed x9, local copies, waits for them, and re-layouts: 12.7 us -> 8.58 us
    pallas_call x1, Pallas kernels: 55.8 us -> 52.8 us  [on_device(): pl.pallas_call(functools.partial(layer_kernel, n, nch, yl, scale), out_sh...]
where the time goes in v4:
time: 62.9 us; the launch traced here: 62.7 us
  Pallas kernels  52.8 us (84%)
  local copies, waits for them, and re-layouts  8.58 us (14%)
  between operations  1.3 us (2%)
    pallas_call x1, Pallas kernels, on_device(): pl.pallas_call(functools.partial(layer_kernel, n, nch, yl, scale), out_sh...  52.8 us
    unnamed x9, local copies, waits for them, and re-layouts  8.58 us

profile of v4, /device:TPU:0, one launch (start us, length us, event | category | flops | bytes accessed | tf_op | source)
XLA Modules:
  0.0 62.7 jit_solution(9862250550059297634)
XLA Ops:
  1.3 0.0 copy-start
  1.3 2.1 %copy-done = bf16[27,192,384]{2,1,0:T(8,128)(2,1)S(1)} copy-done((bf16[27,192,384]{2,1,0:T(8,128)(2,1)S(1)}, bf16[27,192,384]{2,1,0:T(8,128)(2,1)}, u32[]{:S(2)}) %copy-start) | copy-done | bytes 3981336
  3.4 0.0 copy-start.1
  3.4 0.9 %copy-done.1 = bf16[192,2,2,128]{3,2,1,0:T(2,128)(2,1)S(1)} copy-done((bf16[192,2,2,128]{3,2,1,0:T(2,128)(2,1)S(1)}, bf16[192,2,2,128]{3,2,1,0:T(2,128)(2,1)}, u32[]{:S(2)}) %copy-start.1) | copy-done | bytes 196632
  4.3 0.0 copy-start.2
  4.3 0.9 %copy-done.2 = bf16[192,2,2,128]{3,2,1,0:T(2,128)(2,1)S(1)} copy-done((bf16[192,2,2,128]{3,2,1,0:T(2,128)(2,1)S(1)}, bf16[192,2,2,128]{3,2,1,0:T(2,128)(2,1)}, u32[]{:S(2)}) %copy-start.2) | copy-done | bytes 196632
  5.3 52.8 %layer.1 = (bf16[192,2,2,128]{3,2,1,0:T(2,128)(2,1)S(1)}, bf16[192,2,2,128]{3,2,1,0:T(2,128)(2,1)S(1)}, f32[27,192,384]{2,1,0:T(8,128)S(1)}) custom-call(s32[1]{0:T(128)S(6)} %copy.10.shear_ref, bf16[192,2,2,128]{3,2,1,0:T(2,128)(2,1)S(1)} %copy-done.1, bf16[192,2,2,128]{3,2,1,0:T(2,128)(2,1)S(1)} %copy-done.2, bf16[27,192,384]{2,1,0:T(8,128)(2,1)S(1)} %copy-done), custom_call_target="tpu_custom_call" | custom-call | tf_op jit(solution)/shard_map/layer/pallas_call | solution.py:457
  58.1 0.7 %copy.11 = bf16[192,2,2,128]{3,2,1,0:T(2,128)(2,1)} copy(bf16[192,2,2,128]{3,2,1,0:T(2,128)(2,1)S(1)} %get-tuple-element.6) | data formatting | bytes 393216
  58.8 0.7 %copy.12 = bf16[192,2,2,128]{3,2,1,0:T(2,128)(2,1)} copy(bf16[192,2,2,128]{3,2,1,0:T(2,128)(2,1)S(1)} %get-tuple-element.7) | data formatting | bytes 393216
  59.5 3.3 %copy.13 = f32[27,192,384]{2,1,0:T(8,128)} copy(f32[27,192,384]{2,1,0:T(8,128)S(1)} %get-tuple-element.8) | data formatting | bytes 15925248
Async XLA Ops:
  1.3 2.1 %copy-start = (bf16[27,192,384]{2,1,0:T(8,128)(2,1)S(1)}, bf16[27,192,384]{2,1,0:T(8,128)(2,1)}, u32[]{:S(2)}) copy-start(bf16[27,192,384]{2,1,0:T(8,128)(2,1)} %w_ref.1) | copy-start | bytes 11943940
  3.4 0.9 %copy-start.1 = (bf16[192,2,2,128]{3,2,1,0:T(2,128)(2,1)S(1)}, bf16[192,2,2,128]{3,2,1,0:T(2,128)(2,1)}, u32[]{:S(2)}) copy-start(bf16[192,2,2,128]{3,2,1,0:T(2,128)(2,1)} %a_ref.1) | copy-start | bytes 589828
  4.3 0.9 %copy-start.2 = (bf16[192,2,2,128]{3,2,1,0:T(2,128)(2,1)S(1)}, bf16[192,2,2,128]{3,2,1,0:T(2,128)(2,1)}, u32[]{:S(2)}) copy-start(bf16[192,2,2,128]{3,2,1,0:T(2,128)(2,1)} %t_ref.1) | copy-start | bytes 589828
